TPU v7x, 32 devices: a whole 2x2x4 slice. The times are simulated.
32 devices in a mesh: node: 4 (over y, x), grid: 8 (over z, core).
Axes of the slice: x: 2, y: 2, z: 4, core: 2. Of those that a mesh axis runs over, the one named last changes fastest.
Arguments:
- probes: float32 [1, 48, 192, 256], P(None, 'grid'), may hold values from -6 to 6
- potential: float32 [48, 192, 256], P('grid'), may hold values from -2 to 1
- warm_start: bfloat16 [4, 1, 2, 48, 192, 256], P('node', None, None, 'grid'), may hold values from -0.29882812 to 0.29882812
- shift_points: float32 [4, 2], P('node'), may hold values from -4 to 9, as said below
- quad_weights: float32 [4, 2], P('node'), may hold values from -0.3 to 0.3
Outputs:
- moments: float32 [2, 1, 2, 48, 192, 256], P(None, None, None, 'grid', 'node')
- trace_estimate: float32 [2], replicated
Inputs may be any that keep to these rules, and one draw needn't show every extreme that they name: `shift_points`: column 0 holds real parts in -1 to 9; column 1 holds imaginary parts whose magnitude lies in 1 to 4.
All inputs are finite; a program needn't handle non-finite values.
Results may differ from a plain program's by a relative error of at most 0.0003.
Values may be sent and summed in bfloat16 or wider, within the bound.
A program may use at most 192 MiB of HBM per device.

v0:
```python
import jax
import jax.numpy as jnp
from jax import lax
from jax.sharding import PartitionSpec as P

PROBES = 1
ITERS = 2
MOMENTS = 2


near_weight = 4.0 / 3.0
far_weight = -1.0 / 12.0
self_weight = -7.5


def with_halo(cells, sides, width):
    for axis, dim in sides:
        count = lax.axis_size(axis)
        head = lax.slice_in_dim(cells, 0, width, axis=dim)
        tail = lax.slice_in_dim(cells, cells.shape[dim] - width, cells.shape[dim], axis=dim)
        cells = jnp.concatenate(
            [
                lax.ppermute(tail, axis, [(i, (i + 1) % count) for i in range(count)]),
                cells,
                lax.ppermute(head, axis, [((i + 1) % count, i) for i in range(count)]),
            ],
            axis=dim,
        )
    return cells


def hamiltonian_apply(padded, potential, shift_real, shift_imag):
    middle = padded[:, :, :, 2:-2]
    near_sum = (
        padded[:, :, :, 1:-3]
        + padded[:, :, :, 3:-1]
        + (jnp.roll(middle, 1, 4) + jnp.roll(middle, -1, 4))
        + (jnp.roll(middle, 1, 5) + jnp.roll(middle, -1, 5))
    )
    far_sum = (
        padded[:, :, :, :-4]
        + padded[:, :, :, 4:]
        + (jnp.roll(middle, 2, 4) + jnp.roll(middle, -2, 4))
        + (jnp.roll(middle, 2, 5) + jnp.roll(middle, -2, 5))
    )
    laplacian = near_weight * near_sum + far_weight * far_sum + self_weight * middle
    real_shift = shift_real[:, None, None, None, None]
    imag_shift = shift_imag[:, None, None, None, None]
    real_part = middle[:, :, 0]
    imag_part = middle[:, :, 1]
    result_real = (
        real_shift * real_part
        - imag_shift * imag_part
        + 0.5 * laplacian[:, :, 0]
        - potential * real_part
    )
    result_imag = (
        real_shift * imag_part
        + imag_shift * real_part
        + 0.5 * laplacian[:, :, 1]
        - potential * imag_part
    )
    return jnp.stack([result_real, result_imag], axis=2)


def bilinear(first_vec, second_vec):
    real_sum = jnp.sum(
        first_vec[:, :, 0] * second_vec[:, :, 0] - first_vec[:, :, 1] * second_vec[:, :, 1],
        axis=(2, 3, 4),
    )
    imag_sum = jnp.sum(
        first_vec[:, :, 0] * second_vec[:, :, 1] + first_vec[:, :, 1] * second_vec[:, :, 0],
        axis=(2, 3, 4),
    )
    return jnp.stack([real_sum, imag_sum], axis=-1)


def complex_times(factor_one, factor_two):
    return jnp.stack(
        [
            factor_one[..., 0] * factor_two[..., 0] - factor_one[..., 1] * factor_two[..., 1],
            factor_one[..., 0] * factor_two[..., 1] + factor_one[..., 1] * factor_two[..., 0],
        ],
        axis=-1,
    )


def complex_divide(factor_one, factor_two):
    magnitude = factor_two[..., 0] * factor_two[..., 0] + factor_two[..., 1] * factor_two[..., 1]
    return jnp.stack(
        [
            (factor_one[..., 0] * factor_two[..., 0] + factor_one[..., 1] * factor_two[..., 1])
            / magnitude,
            (factor_one[..., 1] * factor_two[..., 0] - factor_one[..., 0] * factor_two[..., 1])
            / magnitude,
        ],
        axis=-1,
    )


def scale_field(scalars, vector):
    real_scalar = scalars[..., 0][:, :, None, None, None]
    imag_scalar = scalars[..., 1][:, :, None, None, None]
    return jnp.stack(
        [
            real_scalar * vector[:, :, 0] - imag_scalar * vector[:, :, 1],
            real_scalar * vector[:, :, 1] + imag_scalar * vector[:, :, 0],
        ],
        axis=2,
    )


def trim_planes(vector, extent_now, extent_out, along_dim):
    excess = extent_now - extent_out
    if excess == 0:
        return vector
    return lax.slice_in_dim(vector, excess, vector.shape[along_dim] - excess, axis=along_dim)


def center(vector, extent):
    return trim_planes(vector, extent, 0, 3)


def residual_norms(vector):
    return lax.psum(bilinear(vector, vector), "grid")


def per_device(probes, potential, warm_start, shift_points, quad_weights):
    shift_real = shift_points[:, 0]
    shift_imag = shift_points[:, 1]
    start_width = 2
    start_wide = with_halo(warm_start, (("grid", 3),), start_width).astype(jnp.float32)
    start_extent = start_width - 2
    solution = warm_start.astype(jnp.float32)
    potential_extent = 0
    source = jnp.stack([probes, jnp.zeros_like(probes)], axis=1)[None]
    residual = source - hamiltonian_apply(
        start_wide,
        trim_planes(potential, potential_extent, start_extent, 0),
        shift_real,
        shift_imag,
    )
    direction = residual
    extent = start_extent
    residual_extent = start_extent
    norm_now = residual_norms(center(residual, start_extent))
    for iteration in range(ITERS):
        padded = with_halo(direction, (("grid", 3),), 2)
        margin = 2
        extent_out = margin - 2
        applied = hamiltonian_apply(
            padded, trim_planes(potential, potential_extent, extent_out, 0), shift_real, shift_imag
        )
        applied, direction, extent = (
            applied,
            trim_planes(padded, margin, extent_out, 3),
            extent_out,
        )
        if iteration == 0:
            residual = direction
            residual_extent = extent
        center_part = center(direction, extent)
        curvature = lax.psum(bilinear(center_part, center(applied, extent)), "grid")
        step_length = complex_divide(norm_now, curvature)
        solution = solution + scale_field(step_length, center_part)
        residual = trim_planes(residual, residual_extent, extent, 3) - scale_field(
            step_length, applied
        )
        residual_extent = extent
        if iteration + 1 < ITERS:
            norm_next = residual_norms(center(residual, extent))
            direction = residual + scale_field(complex_divide(norm_next, norm_now), direction)
            norm_now = norm_next
    scaled_shift = jnp.stack([(shift_real - 4.0) / 5.0, shift_imag / 5.0], axis=-1)
    weight_power = quad_weights
    powers = []
    for degree in range(MOMENTS):
        powers.append(weight_power)
        weight_power = complex_times(weight_power, scaled_shift)
    coefficients = jnp.stack(powers)
    coef_real = coefficients[..., 0]
    coef_imag = coefficients[..., 1]
    highest = lax.Precision.HIGHEST
    sol_real = solution[:, :, 0]
    sol_imag = solution[:, :, 1]
    term_real = jnp.einsum("ks,spzxy->kpzxy", coef_real, sol_real, precision=highest) - jnp.einsum(
        "ks,spzxy->kpzxy", coef_imag, sol_imag, precision=highest
    )
    term_imag = jnp.einsum("ks,spzxy->kpzxy", coef_real, sol_imag, precision=highest) + jnp.einsum(
        "ks,spzxy->kpzxy", coef_imag, sol_real, precision=highest
    )
    moment_terms = jnp.stack([term_real, term_imag], axis=2)
    moments = lax.psum_scatter(moment_terms, "node", scatter_dimension=4, tiled=True)
    inner_sums = jnp.einsum("pzxy,spczxy->sc", probes, solution, precision=highest) / PROBES
    local_trace = jnp.sum(complex_times(quad_weights, inner_sums), axis=0)
    trace_estimate = lax.psum(local_trace, ("node", "grid"))
    return (moments, trace_estimate)


def solution(mesh):
    return jax.shard_map(
        per_device,
        mesh=mesh,
        in_specs=(
            P(None, "grid", None, None),
            P("grid", None, None),
            P("node", None, None, "grid", None, None),
            P("node", None),
            P("node", None),
        ),
        out_specs=(P(None, None, None, "grid", "node", None), P()),
        check_vma=False,
    )
```

profile of v0, /device:TPU:0, one launch (start us, length us, event | category | flops | bytes accessed | tf_op | source)
XLA Modules:
  0.0 308.0 jit_solution(7874606106377025501)
XLA Ops:
  7.2 1.3 fusion.100
  8.5 4.5 %collective-permute-start.1 = (bf16[1,1,2,2,192,256]{5,4,3,2,1,0:T(8,128)(2,1)S(1)}, bf16[1,1,2,2,192,256]{5,4,3,2,1,0:T(8,128)(2,1)S(1)}, u32[]{:S(2)}, u32[]{:S(2)}) collective-permute-start(bf16[1,1,2,2,192,256]{5,4,3,2,1,0:T(8,128)(2,1)S(1)} %get-tuple-element.85), channel_id=1, source_target_pairs={{1,0},{2,1},{3,2},{4,3},{5,4},{6,5},{7,6},{0,7},{9,8},{10,9},{11,1... | collective-permute-start | bytes 1179656 | tf_op jit(solution)/shard_map/ppermute | solution.py:25
  13.0 1.4 fusion.107
  15.8 1.3 fusion.102
  19.6 1.0 collective-permute-done.1
  20.6 2.9 collective-permute-done
  23.8 0.5 fusion.81
  24.4 2.2 fusion.79
  26.6 1.4 fusion.80
  28.0 2.6 fusion.78
  30.6 2.9 fusion.76
  33.5 1.8 fusion.77
  35.4 8.3 %fusion.24 = f32[1,1,2,6,192,256]{5,4,3,2,1,0:T(8,128)} fusion(f32[1,1,2,10,192,256]{5,4,3,2,1,0:T(8,128)S(1)} %maximum_convert_fusion, f32[1,1,2,6,191,256]{5,4,3,2,1,0:T(8,128)S(1)} %get-tuple-element.31, f32[1,1,2,6,1,256]{5,4,3,2,1,0:T(1,128)S(1)} %get-tuple-element.83, f32[1,1,2,6,1,256]{5,4,3,2,1,0:T(1,128)S(1)} %get-tuple-element.82, ...), kind=kLoop, calls=%fused_computation.38 | loop fusion | flops 13565952 | bytes 33030144 | tf_op jit(solution)/shard_map/add | solution.py:46
  43.7 3.6 %fusion.54 = (f32[1,1,1,6,192,256]{5,4,3,2,1,0:T(8,128)S(1)}, f32[1,1,1,6,192,256]{5,4,3,2,1,0:T(8,128)S(1)}) fusion(f32[1,1,2,6,192,256]{5,4,3,2,1,0:T(8,128)} %fusion.24, f32[6,192,256]{2,1,0:T(8,128)S(1)} %copy-done.7, f32[1,1,2,10,192,256]{5,4,3,2,1,0:T(8,128)S(1)} %maximum_convert_fusion, f32[]{:T(128)} %bitcast.6, f32[]{:T(128)} %bitcast.4), kind=kLoop, calls=%fused_computation.97 | loop fusion | flops 4128768 | bytes 8257544 | tf_op jit(solution)/shard_map/stack | solution.py:63
  47.5 0.7 copy-done.1
  48.8 1.8 fusion.97
  50.6 3.0 fusion.95
  53.6 1.4 fusion.96
  55.0 1.8 fusion.92
  56.9 1.0 subtract_reduce_fusion.1
  57.8 0.9 collective-permute-start.3
  58.7 1.9 pad_maximum_fusion.6
  60.6 2.6 fusion.93
  63.2 2.9 fusion.91
  66.2 9.4 %collective-permute-done.3 = f32[1,1,2,2,192,256]{5,4,3,2,1,0:T(8,128)S(1)} collective-permute-done((f32[1,1,2,2,192,256]{5,4,3,2,1,0:T(8,128)S(1)}, f32[1,1,2,2,192,256]{5,4,3,2,1,0:T(8,128)S(1)}, u32[]{:S(2)}, u32[]{:S(2)}) %collective-permute-start.3) | collective-permute-done | bytes 786464 | tf_op jit(solution)/shard_map/ppermute | solution.py:25
  75.6 2.1 collective-permute-done.2
  77.8 0.9 copy-done.24
  78.7 9.1 %fusion.14 = f32[1,1,2,6,192,256]{5,4,3,2,1,0:T(8,128)S(1)} fusion(f32[1,1,2,6,192,256]{5,4,3,2,1,0:T(8,128)S(1)} %maximum_subtract_fusion, f32[1,1,2,2,192,256]{5,4,3,2,1,0:T(8,128)} %copy-done.23, f32[1,1,2,2,192,256]{5,4,3,2,1,0:T(8,128)} %copy-done.24, f32[1,1,2,6,191,256]{5,4,3,2,1,0:T(8,128)} %get-tuple-element.75, ...), kind=kLoop, calls=%fused_computation.23 | loop fusion | flops 15925248 | bytes 25165824 | tf_op jit(solution)/shard_map/add | solution.py:46
  87.8 4.3 %fusion.64 = (f32[]{:T(128)}, f32[]{:T(128)}, f32[6,192,256]{2,1,0:T(8,128)}, f32[6,192,256]{2,1,0:T(8,128)}) fusion(f32[1,1,2,6,192,256]{5,4,3,2,1,0:T(8,128)S(1)} %maximum_subtract_fusion, f32[6,192,256]{2,1,0:T(8,128)S(1)} %copy-done.7, f32[1,1,2,6,192,256]{5,4,3,2,1,0:T(8,128)S(1)} %fusion.14, f32[]{:T(128)} %bitcast.6, f32[]{:T(128)} %bitcast.4), kind=kLoop, calls=%fused_computation.124 | loop fusion | flops 6488062 | bytes 8257552 | tf_op jit(solution)/shard_map/reduce_sum | solution.py:67
  92.1 1.8 pad_maximum_fusion.7
  93.9 15.5 %all-reduce.1 = (f32[1,1,2]{2,1,0:T(1,128)S(1)}, f32[1,1,2]{2,1,0:T(1,128)S(1)}) all-reduce(f32[1,1,2]{2,1,0:T(1,128)S(1)} %copy-done.28, f32[1,1,2]{2,1,0:T(1,128)} %pad_maximum_fusion.7), channel_id=1, replica_groups=mesh['node'=4,'grid'=8] {'grid'}, use_global_device_ids=true, to_apply=%region_2.3 | all-reduce | flops 4 | bytes 32 | tf_op jit(solution)/shard_map/psum | solution.py:125
  109.5 0.7 fusion.105
  119.2 2.1 subtract_bitcast_fusion.1
  122.4 0.5 copy-done.11
  122.9 1.0 subtract_reduce_fusion
  123.9 1.3 pad_maximum_fusion.8
  126.5 13.6 %psum.37 = f32[1,1,2]{2,1,0:T(1,128)S(1)} all-reduce(f32[1,1,2]{2,1,0:T(1,128)S(1)} %pad_maximum_fusion.8), channel_id=1, replica_groups=mesh['node'=4,'grid'=8] {'grid'}, use_global_device_ids=true, to_apply=%region_8.9 | all-reduce | flops 2 | bytes 16 | tf_op jit(solution)/shard_map/psum | solution.py:125
  140.1 0.7 fusion.104
  146.0 1.9 multiply_subtract_fusion.1
  148.0 0.8 copy-done.10
  149.5 0.5 maximum_add_fusion.9
  150.7 3.0 fusion.86
  153.7 1.4 fusion.87
  155.1 1.8 fusion.83
  157.5 2.6 fusion.84
  160.1 2.9 fusion.82
  163.0 11.0 %collective-permute-done.5 = f32[1,1,2,2,192,256]{5,4,3,2,1,0:T(8,128)S(1)} collective-permute-done((f32[1,1,2,2,192,256]{5,4,3,2,1,0:T(8,128)S(1)}, f32[1,1,2,2,192,256]{5,4,3,2,1,0:T(8,128)S(1)}, u32[]{:S(2)}, u32[]{:S(2)}) %collective-permute-start.5) | collective-permute-done | bytes 786464 | tf_op jit(solution)/shard_map/ppermute | solution.py:25
  174.0 0.8 collective-permute-done.4
  174.9 0.8 copy-done.26
  175.7 9.9 %fusion.6 = f32[1,1,2,6,192,256]{5,4,3,2,1,0:T(8,128)} fusion(f32[1,1,2,6,192,256]{5,4,3,2,1,0:T(8,128)S(1)} %maximum_add_fusion.9, f32[1,1,2,2,192,256]{5,4,3,2,1,0:T(8,128)} %copy-done.25, f32[1,1,2,2,192,256]{5,4,3,2,1,0:T(8,128)} %copy-done.26, f32[1,1,2,6,191,256]{5,4,3,2,1,0:T(8,128)S(1)} %get-tuple-element.51, ...), kind=kLoop, calls=%fused_computation.15 | loop fusion | flops 15925248 | bytes 25165824 | tf_op jit(solution)/shard_map/add | solution.py:46
  185.6 3.5 %fusion.40 = (f32[6,192,256]{2,1,0:T(8,128)S(1)}, f32[6,192,256]{2,1,0:T(8,128)S(1)}) fusion(f32[1,1,2,6,192,256]{5,4,3,2,1,0:T(8,128)} %fusion.6, f32[6,192,256]{2,1,0:T(8,128)S(1)} %copy-done.8, f32[1,1,2,6,192,256]{5,4,3,2,1,0:T(8,128)S(1)} %maximum_add_fusion.9, f32[]{:T(128)} %bitcast.6, f32[]{:T(128)} %bitcast.4), kind=kLoop, calls=%fused_computation.79 | loop fusion | flops 4128768 | bytes 8257544 | tf_op jit(solution)/shard_map/sub | solution.py:52
  189.1 1.2 fusion.58
  190.3 2.0 pad_maximum_fusion.9
  192.5 16.9 %psum.38 = f32[1,1,2]{2,1,0:T(1,128)S(1)} all-reduce(f32[1,1,2]{2,1,0:T(1,128)} %pad_maximum_fusion.9), channel_id=1, replica_groups=mesh['node'=4,'grid'=8] {'grid'}, use_global_device_ids=true, to_apply=%region_11.12 | all-reduce | flops 2 | bytes 16 | tf_op jit(solution)/shard_map/psum | solution.py:163
  209.4 0.6 fusion.103
  218.2 1.0 copy-done.21
  219.1 1.2 copy-done.22
  220.9 0.7 subtract_bitcast_fusion
  221.6 2.6 pad_maximum_fusion
  224.2 1.2 copy-done.14
  225.8 2.1 fusion.108
  227.9 29.6 %fusion.68 = f32[1,2]{1,0:T(1,128)S(1)} fusion(f32[6,192,256,1]{2,1,0,3:T(8,128)S(1)} %bitcast.197, f32[2,6,192,256]{3,2,1,0:T(8,128)S(1)} %fusion.108), kind=kOutput, calls=%fused_computation.145 | convolution fusion | flops 7077888 | bytes 3538952 | tf_op jit(solution)/shard_map/pzxy,spczxy->sc/dot_general | solution.py:194
  257.5 0.6 fusion.101
  263.1 38.1 %psum.39 = f32[2]{0:T(128)} all-reduce(f32[2]{0:T(128)S(1)} %maximum_bitcast_fusion.1), channel_id=1, replica_groups=mesh['node'=4,'grid'=8] {'node','grid'}, use_global_device_ids=true, to_apply=%region_13.14 | all-reduce | flops 2 | bytes 16 | tf_op jit(solution)/shard_map/psum | solution.py:196
  (75 shorter events, 5.7 us)
Async XLA Ops:
  7.2 16.4 %copy-start = (bf16[1,1,2,6,192,256]{5,4,3,2,1,0:T(8,128)(2,1)S(1)}, bf16[1,1,2,6,192,256]{5,4,3,2,1,0:T(8,128)(2,1)}, u32[]{:S(2)}) copy-start(bf16[1,1,2,6,192,256]{5,4,3,2,1,0:T(8,128)(2,1)} %param.7) | copy-start | bytes 3538948
  7.2 294.0 %reduce-scatter.2.cloned.1.call-start = ((), (), s32[]{:S(2)}) async-start(), calls=%async_computation.1 | async-start | bytes 5898240 | tf_op jit(solution)/shard_map/reduce_scatter | solution.py:193
  8.5 12.1 %collective-permute-start.1 = (bf16[1,1,2,2,192,256]{5,4,3,2,1,0:T(8,128)(2,1)S(1)}, bf16[1,1,2,2,192,256]{5,4,3,2,1,0:T(8,128)(2,1)S(1)}, u32[]{:S(2)}, u32[]{:S(2)}) collective-permute-start(bf16[1,1,2,2,192,256]{5,4,3,2,1,0:T(8,128)(2,1)S(1)} %get-tuple-element.85), channel_id=1, source_target_pairs={{1,0},{2,1},{3,2},{4,3},{5,4},{6,5},{7,6},{0,7},{9,8},{10,9},{11,1... | collective-permute-start | bytes 1179656 | tf_op jit(solution)/shard_map/ppermute | solution.py:25
  13.0 10.5 %collective-permute-start = (bf16[1,1,2,2,192,256]{5,4,3,2,1,0:T(8,128)(2,1)S(1)}, bf16[1,1,2,2,192,256]{5,4,3,2,1,0:T(8,128)(2,1)S(1)}, u32[]{:S(2)}, u32[]{:S(2)}) collective-permute-start(bf16[1,1,2,2,192,256]{5,4,3,2,1,0:T(8,128)(2,1)S(1)} %get-tuple-element.84), channel_id=1, source_target_pairs={{0,1},{1,2},{2,3},{3,4},{4,5},{5,6},{6,7},{7,0},{8,9},{9,10},{10,1... | collective-permute-start | bytes 1179656 | tf_op jit(solution)/shard_map/ppermute | solution.py:23
  35.4 8.3 %copy-start.7 = (f32[6,192,256]{2,1,0:T(8,128)S(1)}, f32[6,192,256]{2,1,0:T(8,128)}, u32[]{:S(2)}) copy-start(f32[6,192,256]{2,1,0:T(8,128)} %param.6) | copy-start | bytes 3538948
  43.7 3.6 %copy-start.17 = (f32[1,6,192,256]{3,2,1,0:T(8,128)S(1)}, f32[1,6,192,256]{3,2,1,0:T(8,128)}, u32[]{:S(2)}) copy-start(f32[1,6,192,256]{3,2,1,0:T(8,128)} %param.5) | copy-start | bytes 3538948
  47.3 1.0 copy-start.1
  47.3 1.4 copy-start.4
  57.8 17.8 %collective-permute-start.3 = (f32[1,1,2,2,192,256]{5,4,3,2,1,0:T(8,128)S(1)}, f32[1,1,2,2,192,256]{5,4,3,2,1,0:T(8,128)S(1)}, u32[]{:S(2)}, u32[]{:S(2)}) collective-permute-start(f32[1,1,2,2,192,256]{5,4,3,2,1,0:T(8,128)S(1)} %get-tuple-element.79), channel_id=1, source_target_pairs={{1,0},{2,1},{3,2},{4,3},{5,4},{6,5},{7,6},{0,7},{9,8},{10,9},{11,1... | collective-permute-start | bytes 2359304 | tf_op jit(solution)/shard_map/ppermute | solution.py:25
  58.7 19.0 %collective-permute-start.2 = (f32[1,1,2,2,192,256]{5,4,3,2,1,0:T(8,128)S(1)}, f32[1,1,2,2,192,256]{5,4,3,2,1,0:T(8,128)S(1)}, u32[]{:S(2)}, u32[]{:S(2)}) collective-permute-start(f32[1,1,2,2,192,256]{5,4,3,2,1,0:T(8,128)S(1)} %get-tuple-element.78), channel_id=1, source_target_pairs={{0,1},{1,2},{2,3},{3,4},{4,5},{5,6},{6,7},{7,0},{8,9},{9,10},{10,1... | collective-permute-start | bytes 2359304 | tf_op jit(solution)/shard_map/ppermute | solution.py:23
  75.6 2.1 copy-start.23
  77.7 0.9 copy-start.24
  87.8 6.2 %copy-start.28 = (f32[1,1,2]{2,1,0:T(1,128)S(1)}, f32[1,1,2]{2,1,0:T(1,128)}, u32[]{:S(2)}) copy-start(f32[1,1,2]{2,1,0:T(1,128)} %pad_maximum_fusion.6) | copy-start | bytes 28
  119.2 2.2 copy-start.2
  119.2 2.3 copy-start.5
  119.2 2.7 copy-start.18
  121.3 1.0 copy-start.9
  121.3 1.6 copy-start.11
  146.0 2.0 copy-start.3
  146.0 2.0 copy-start.6
  146.0 2.8 copy-start.10
  146.0 3.2 %copy-start.12 = (f32[1,1,1,6,192,256]{5,4,3,2,1,0:T(8,128)S(1)}, f32[1,1,1,6,192,256]{5,4,3,2,1,0:T(8,128)}, u32[]{:S(2)}) copy-start(f32[1,1,1,6,192,256]{5,4,3,2,1,0:T(8,128)} %copy-done.11) | copy-start | bytes 3538948
  146.0 3.5 %copy-start.19 = (f32[1,6,192,256]{3,2,1,0:T(8,128)S(1)}, f32[1,6,192,256]{3,2,1,0:T(8,128)}, u32[]{:S(2)}) copy-start(f32[1,6,192,256]{3,2,1,0:T(8,128)} %param.5) | copy-start | bytes 3538948
  156.9 17.0 %collective-permute-start.5 = (f32[1,1,2,2,192,256]{5,4,3,2,1,0:T(8,128)S(1)}, f32[1,1,2,2,192,256]{5,4,3,2,1,0:T(8,128)S(1)}, u32[]{:S(2)}, u32[]{:S(2)}) collective-permute-start(f32[1,1,2,2,192,256]{5,4,3,2,1,0:T(8,128)S(1)} %get-tuple-element.55), channel_id=1, source_target_pairs={{1,0},{2,1},{3,2},{4,3},{5,4},{6,5},{7,6},{0,7},{9,8},{10,9},{11,1... | collective-permute-start | bytes 2359304 | tf_op jit(solution)/shard_map/ppermute | solution.py:25
  156.9 17.8 %collective-permute-start.4 = (f32[1,1,2,2,192,256]{5,4,3,2,1,0:T(8,128)S(1)}, f32[1,1,2,2,192,256]{5,4,3,2,1,0:T(8,128)S(1)}, u32[]{:S(2)}, u32[]{:S(2)}) collective-permute-start(f32[1,1,2,2,192,256]{5,4,3,2,1,0:T(8,128)S(1)} %get-tuple-element.54), channel_id=1, source_target_pairs={{0,1},{1,2},{2,3},{3,4},{4,5},{5,6},{6,7},{7,0},{8,9},{9,10},{10,1... | collective-permute-start | bytes 2359304 | tf_op jit(solution)/shard_map/ppermute | solution.py:23
  174.0 0.9 copy-start.25
  174.8 0.9 copy-start.26
  175.7 9.9 %copy-start.8 = (f32[6,192,256]{2,1,0:T(8,128)S(1)}, f32[6,192,256]{2,1,0:T(8,128)}, u32[]{:S(2)}) copy-start(f32[6,192,256]{2,1,0:T(8,128)} %param.6) | copy-start | bytes 3538948
  189.1 3.2 %copy-start.27 = (f32[1,2]{1,0:T(1,128)S(1)}, f32[1,2]{1,0:T(1,128)}, u32[]{:S(2)}) copy-start(f32[1,2]{1,0:T(1,128)} %param.9) | copy-start | bytes 28
  217.8 1.3 copy-start.21
  217.8 2.5 copy-start.22
  218.1 2.6 copy-start.13
  218.1 2.6 copy-start.15
  224.2 1.3 copy-start.14
  224.2 1.6 copy-start.16
  225.8 2.1 copy-start.20
Sparse Core Ops, SparseCore 0:
  224.3 55.9 reduce-scatter.1
where the time goes:
time: 310 us; the launch traced here: 308 us
  blocking collectives  84.1 us (27%)
  other arithmetic  60.8 us (20%)
  local copies, waits for them, and re-layouts  53.7 us (17%)
  between operations  46.6 us (15%)
  matrix products  29.6 us (10%)
  waiting for transfers between devices  27.3 us (9%)
  starting transfers between devices  5.97 us (2%)
    psum x1, blocking collectives, per_device(): trace_estimate = lax.psum(local_trace, ('node', 'grid'))  38.1 us
    dot_general x1, matrix products, per_device(): jnp.einsum('pzxy,spczxy->sc', probes, solution, precision=highest) / PROBES  29.6 us
    psum x2, blocking collectives, residual_norms(): return lax.psum(bilinear(vector, vector), 'grid')  29.1 us
    add x3, other arithmetic, hamiltonian_apply(): near_weight * near_sum + far_weight * far_sum + self_weight * middle  27.3 us
    ppermute x3, waiting for transfers between devices, with_halo(): lax.ppermute(head, axis, [((i + 1) % count, i) for i in range(count)])  21.4 us
    psum x1, blocking collectives, per_device(): curvature = lax.psum(bilinear(center_part, center(applied, extent)), 'grid')  16.9 us
    slice x6, local copies, waits for them, and re-layouts, hamiltonian_apply(): jnp.roll(middle, -2, 5)  14.3 us
    slice x6, local copies, waits for them, and re-layouts, hamiltonian_apply(): jnp.roll(middle, -1, 5)  12.4 us
  transfers between devices with their start and end apart: 7, of which 6 were waited for; matrix products, arithmetic and copies ran while one was open for 16% of the time, Pallas kernels for 0%

commit v1 on v0

v1 whole, which is shorter than its diff:
```python
import functools

import jax
import jax.numpy as jnp
import ml_dtypes
import numpy as np
from jax import lax
from jax.experimental import pallas as pl
from jax.experimental.pallas import tpu as pltpu
from jax.sharding import PartitionSpec as P

MESH = pl.DeviceIdType.MESH
SUMS = 16
CHUNK = 32


def ring_matrix(size, diagonal):
    matrix = np.zeros((size, size), np.float32)
    at = np.arange(size)
    for step, weight in ((1, 16.0), (2, -1.0)):
        matrix[at, (at + step) % size] += weight
        matrix[at, (at - step) % size] += weight
    matrix[at, at] += diagonal
    return matrix.astype(ml_dtypes.bfloat16)


def cmul(a, b):
    return a[0] * b[0] - a[1] * b[1], a[0] * b[1] + a[1] * b[0]


def cdiv(a, b):
    size = b[0] * b[0] + b[1] * b[1]
    return (a[0] * b[0] + a[1] * b[1]) / size, (a[1] * b[0] - a[0] * b[1]) / size


def fold(values):
    rows, cols = values.shape
    return jnp.sum(values.reshape(rows // 8, 8, cols), axis=0)


def kernel(
    nodes,
    slabs,
    warm,
    probes,
    potential,
    shift_ref,
    weight_ref,
    along_x,
    along_y,
    moments,
    trace,
    xbuf,
    bbuf,
    vbuf,
    rbuf,
    qbuf,
    qlow,
    plane,
    acc,
    sums,
    final,
    arrived,
    notes,
    local_sem,
    x_send,
    x_recv,
    r_send,
    r_recv,
    q_send,
    q_recv,
    s_send,
    s_recv,
    n_send,
    n_recv,
    f_send,
    f_recv,
):
    node, slab = lax.axis_index("node"), lax.axis_index("grid")
    depth, width, length = bbuf.shape
    half = width // 2
    block = width // nodes
    above = (node, lax.rem(slab + 1, slabs))
    below = (node, lax.rem(slab + slabs - 1, slabs))

    loads = [
        pltpu.make_async_copy(warm.at[0, 0], xbuf.at[:, 2 : depth + 2], local_sem.at[0]),
        pltpu.make_async_copy(probes.at[0], bbuf, local_sem.at[1]),
        pltpu.make_async_copy(potential, vbuf, local_sem.at[2]),
    ]
    for load in loads:
        load.start()

    barrier = pltpu.get_barrier_semaphore()
    for k in range(1, slabs):
        pl.semaphore_signal(
            barrier, inc=1, device_id=(node, lax.rem(slab + k, slabs)), device_id_type=MESH
        )
    for k in range(1, nodes):
        pl.semaphore_signal(
            barrier, inc=1, device_id=(lax.rem(node + k, nodes), slab), device_id_type=MESH
        )
    pl.semaphore_wait(barrier, slabs + nodes - 2)

    def send(source, target, send_sem, recv_sem, device):
        copy = pltpu.make_async_remote_copy(
            src_ref=source,
            dst_ref=target,
            send_sem=send_sem,
            recv_sem=recv_sem,
            device_id=device,
            device_id_type=MESH,
        )
        copy.start()
        return copy

    x_down = send(
        warm.at[0, 0, :, 0:2], xbuf.at[:, depth + 2 : depth + 4], x_send.at[0], x_recv.at[0], below
    )
    x_up = send(warm.at[0, 0, :, depth - 2 : depth], xbuf.at[:, 0:2], x_send.at[1], x_recv.at[1], above)

    acc[...] = jnp.zeros_like(acc)
    qbuf[:, depth : depth + 2, half:, :] = jnp.zeros((2, 2, width - half, length), jnp.float32)
    shift = shift_ref[0, 0], shift_ref[0, 1]
    for load in loads:
        load.wait()

    def dot(a, b):
        return jnp.dot(a, b, preferred_element_type=jnp.float32)

    def in_plane_exact(p):
        for part in range(2):
            field = xbuf[part, p + 2]
            plane[part] = dot(field, along_y[...]) + dot(along_x[...], field)

    def in_plane(source, p):
        for part in range(2):
            field = source[part, p]
            high = field.astype(jnp.bfloat16)
            low = (field - high.astype(jnp.float32)).astype(jnp.bfloat16)
            plane[part] = (dot(high, along_y[...]) + dot(low, along_y[...])) + (
                dot(along_x[...], high) + dot(along_x[...], low)
            )

    def apply(field, stencil, local):
        diagonal = shift[0] - local
        return (
            diagonal * field[0] - shift[1] * field[1] + stencil[0] * (1.0 / 24.0),
            diagonal * field[1] + shift[1] * field[0] + stencil[1] * (1.0 / 24.0),
        )

    def in_chunks(first, terms):
        count = terms[1]

        def step(i, totals):
            rows = pl.ds(pl.multiple_of(i * CHUNK, CHUNK), CHUNK)
            values = terms[0](rows)
            return tuple(total + fold(value) for total, value in zip(totals, values))

        zero = jnp.zeros((8, length), jnp.float32)
        totals = lax.fori_loop(0, width // CHUNK, step, (zero,) * count)
        for i, total in enumerate(totals):
            acc[first + i] += total

    def residual_plane(p, carry):
        in_plane_exact(p)

        def terms(rows):
            stencil, field = [], []
            for part in range(2):
                at = [xbuf[part, p + j, rows, :].astype(jnp.float32) for j in range(5)]
                stencil.append(plane[part, rows, :] + 16.0 * (at[1] + at[3]) - (at[0] + at[4]))
                field.append(at[2])
            source = bbuf[p, rows, :]
            image = apply(field, stencil, vbuf[p, rows, :])
            r = source - image[0], -image[1]
            rbuf[0, p + 2, rows, :] = r[0]
            rbuf[1, p + 2, rows, :] = r[1]
            return (
                r[0] * r[0] - r[1] * r[1],
                2.0 * r[0] * r[1],
                source * field[0],
                source * field[1],
                source * r[0],
                source * r[1],
            )

        in_chunks(0, (terms, 6))
        return carry

    def image_plane(p, carry):
        in_plane(rbuf, p + 2)

        def terms(rows):
            stencil, field = [], []
            for part in range(2):
                at = [rbuf[part, p + j, rows, :] for j in range(5)]
                stencil.append(plane[part, rows, :] + 16.0 * (at[1] + at[3]) - (at[0] + at[4]))
                field.append(at[2])
            source = bbuf[p, rows, :]
            q = apply(field, stencil, vbuf[p, rows, :])
            qbuf[0, p, rows, :] = q[0]
            qbuf[1, p, rows, :] = q[1]
            return (
                *cmul(field, q),
                q[0] * q[0] - q[1] * q[1],
                2.0 * q[0] * q[1],
                source * q[0],
                source * q[1],
            )

        in_chunks(6, (terms, 6))
        return carry

    def energy_plane(p, carry):
        in_plane(qbuf, p)

        def terms(rows):
            stencil, field = [], []
            for part in range(2):
                stencil.append(
                    plane[part, rows, :]
                    + 32.0 * qbuf[part, p + 1, rows, :]
                    - 2.0 * qbuf[part, p + 2, rows, :]
                )
                field.append(qbuf[part, p, rows, :])
            return cmul(field, apply(field, stencil, vbuf[p, rows, :]))

        in_chunks(12, (terms, 2))
        return carry

    with jax.named_scope("residual"):
        lax.fori_loop(2, depth - 2, residual_plane, 0)
        x_up.wait_recv()
        x_down.wait_recv()
        lax.fori_loop(0, 2, residual_plane, 0)
        r_down = send(
            rbuf.at[:, 2:4], rbuf.at[:, depth + 2 : depth + 4], r_send.at[0], r_recv.at[0], below
        )
        lax.fori_loop(depth - 2, depth, residual_plane, 0)
        r_up = send(rbuf.at[:, depth : depth + 2], rbuf.at[:, 0:2], r_send.at[1], r_recv.at[1], above)

    with jax.named_scope("image"):
        lax.fori_loop(2, depth - 2, image_plane, 0)
        r_up.wait_recv()
        lax.fori_loop(0, 2, image_plane, 0)
        q_down = send(
            qbuf.at[:, 0:2, 0:half],
            qbuf.at[:, depth : depth + 2, 0:half],
            q_send.at[0],
            q_recv.at[0],
            below,
        )
        r_down.wait_recv()
        lax.fori_loop(depth - 2, depth, image_plane, 0)
        q_up = send(qbuf.at[:, depth - 2 : depth, half:width], qlow, q_send.at[1], q_recv.at[1], above)

    with jax.named_scope("energy"):
        lax.fori_loop(0, depth - 2, energy_plane, 0)
        q_down.wait_recv()
        lax.fori_loop(depth - 2, depth, energy_plane, 0)
        q_up.wait_recv()

        def crossing(i, totals):
            start = i * CHUNK
            mine = pl.ds(pl.multiple_of(half + start, CHUNK), CHUNK)
            theirs = pl.ds(pl.multiple_of(start, CHUNK), CHUNK)
            near = [qlow[part, 1, theirs, :] for part in range(2)]
            far = [qlow[part, 0, theirs, :] for part in range(2)]
            zeroth = [qbuf[part, 0, mine, :] for part in range(2)]
            first = [qbuf[part, 1, mine, :] for part in range(2)]
            one = cmul(zeroth, [32.0 * near[part] - 2.0 * far[part] for part in range(2)])
            two = cmul(first, near)
            return tuple(
                totals[part] + fold((one[part] - 2.0 * two[part]) * (1.0 / 24.0)) for part in range(2)
            )

        zero = jnp.zeros((8, length), jnp.float32)
        totals = lax.fori_loop(0, half // CHUNK, crossing, (zero, zero))
        acc[12] += totals[0]
        acc[13] += totals[1]

    with jax.named_scope("scalars"):
        partial = jnp.sum(acc[...], axis=1)
        lanes = partial[:, 0:128]
        for at in range(128, length, 128):
            lanes = lanes + partial[:, at : at + 128]
        sums[0] = lanes
        scalar_copies = [
            send(
                sums.at[0],
                sums.at[k],
                s_send.at[k],
                s_recv.at[k],
                (node, lax.rem(slab + k, slabs)),
            )
            for k in range(1, slabs)
        ]
        for copy in scalar_copies:
            copy.wait_recv()
        total = jnp.zeros((SUMS, 128), jnp.float32)
        for owner in range(slabs):
            total = total + sums[lax.rem(slab - owner + slabs, slabs)]
        total = jnp.broadcast_to(jnp.sum(total, axis=1, keepdims=True), (SUMS, length))
        pair = lambda i: (total[i : i + 1], total[i + 1 : i + 2])
        s0, t0, t1, s1, s2, t2, s3 = (pair(i) for i in range(0, 14, 2))
        step0 = cdiv(s0, s1)
        square = cmul(step0, step0)
        norm1 = cmul(square, s2)
        norm1 = norm1[0] - s0[0], norm1[1] - s0[1]
        ratio = cdiv(norm1, s0)
        grow = ratio[0] + 1.0, ratio[1]
        one = cmul(cmul(grow, grow), s1)
        two = cmul(cmul(grow, step0), s2)
        three = cmul(square, s3)
        step1 = cdiv(
            norm1, (one[0] - 2.0 * two[0] + three[0], one[1] - 2.0 * two[1] + three[1])
        )
        coef_r = cmul(step1, grow)
        coef_r = coef_r[0] + step0[0], coef_r[1] + step0[1]
        coef_q = cmul(step1, step0)
        coef_q = -coef_q[0], -coef_q[1]
        inner_r, inner_q = cmul(coef_r, t1), cmul(coef_q, t2)
        inner = t0[0] + inner_r[0] + inner_q[0], t0[1] + inner_r[1] + inner_q[1]
        weight = weight_ref[0, 0], weight_ref[0, 1]
        share = cmul(weight, inner)
        following = cmul(weight, ((shift[0] - 4.0) * 0.2, shift[1] * 0.2))
        row = lax.broadcasted_iota(jnp.int32, (8, 128), 0)
        note = jnp.zeros((8, 128), jnp.float32)
        entries = (*weight, *following, share[0][:, 0:128], share[1][:, 0:128])
        for i, entry in enumerate(entries):
            note = jnp.where(row == i, entry, note)
        notes[0] = note
        note_copies = [
            send(notes.at[0], notes.at[k], n_send.at[k], n_recv.at[k], (lax.rem(node + k, nodes), slab))
            for k in range(1, nodes)
        ]

    with jax.named_scope("solution_planes"):

        def final_plane(p, carry):
            def step(i, inner_carry):
                rows = pl.ds(pl.multiple_of(i * CHUNK, CHUNK), CHUNK)
                r = rbuf[0, p + 2, rows, :], rbuf[1, p + 2, rows, :]
                q = qbuf[0, p, rows, :], qbuf[1, p, rows, :]
                along_r, along_q = cmul(coef_r, r), cmul(coef_q, q)
                for part in range(2):
                    start = xbuf[part, p + 2, rows, :].astype(jnp.float32)
                    final[p, part, rows, :] = start + along_r[part] + along_q[part]
                return inner_carry

            lax.fori_loop(0, width // CHUNK, step, 0)
            return carry

        final_copies = []
        for p in range(depth):
            final_plane(p, 0)
            for k in range(1, nodes):
                peer = lax.rem(node + k, nodes)
                rows = pl.ds(pl.multiple_of(peer * block, 8), block)
                final_copies.append(
                    send(
                        final.at[p, :, rows, :],
                        arrived.at[k, p],
                        f_send.at[k, p],
                        f_recv.at[k, p],
                        (peer, slab),
                    )
                )

    with jax.named_scope("moments"):
        for copy in note_copies:
            copy.wait_recv()
        whole_trace = jnp.zeros((8, 128), jnp.float32)
        for owner in range(nodes):
            whole_trace = whole_trace + notes[lax.rem(node - owner + nodes, nodes)]
        lane = lax.broadcasted_iota(jnp.int32, (8, 128), 1)
        for part in range(2):
            trace[part] = jnp.sum(jnp.where((row == 4 + part) & (lane == 0), whole_trace, 0.0))
        weights = []
        for k in range(nodes):
            wide = jnp.broadcast_to(jnp.sum(jnp.where(lane == 0, notes[k], 0.0), axis=1, keepdims=True), (8, length))
            weights.append([(wide[i : i + 1], wide[i + 1 : i + 2]) for i in (0, 2)])
        own = pl.ds(pl.multiple_of(node * block, 8), block)
        for p in range(depth):
            for copy in final_copies[p * (nodes - 1) : (p + 1) * (nodes - 1)]:
                copy.wait_recv()
            fields = [(final[p, 0, own, :], final[p, 1, own, :])]
            for k in range(1, nodes):
                fields.append((arrived[k, p, 0], arrived[k, p, 1]))
            for degree in range(2):
                terms = [cmul(weights[k][degree], fields[k]) for k in range(nodes)]
                for part in range(2):
                    value = terms[0][part]
                    for term in terms[1:]:
                        value = value + term[part]
                    moments[degree, 0, part, p] = value

    for copy in [x_down, x_up, r_down, r_up, q_down, q_up, *scalar_copies, *note_copies, *final_copies]:
        copy.wait_send()


def per_device(nodes, slabs, probes, potential, warm_start, shift_points, quad_weights):
    depth, width, length = potential.shape
    block = width // nodes
    f32, bf16 = jnp.float32, jnp.bfloat16
    anywhere = pl.BlockSpec(memory_space=pl.ANY)
    scalars = pl.BlockSpec(memory_space=pltpu.SMEM)
    vector = pl.BlockSpec(memory_space=pltpu.VMEM)
    dma = pltpu.SemaphoreType.DMA
    return pl.pallas_call(
        functools.partial(kernel, nodes, slabs),
        out_shape=(
            jax.ShapeDtypeStruct((2, 1, 2, depth, block, length), f32),
            jax.ShapeDtypeStruct((2,), f32),
        ),
        in_specs=[anywhere, anywhere, anywhere, scalars, scalars, vector, vector],
        out_specs=(vector, scalars),
        scratch_shapes=[
            pltpu.VMEM((2, depth + 4, width, length), bf16),
            pltpu.VMEM((depth, width, length), f32),
            pltpu.VMEM((depth, width, length), f32),
            pltpu.VMEM((2, depth + 4, width, length), f32),
            pltpu.VMEM((2, depth + 2, width, length), f32),
            pltpu.VMEM((2, 2, width - width // 2, length), f32),
            pltpu.VMEM((2, width, length), f32),
            pltpu.VMEM((SUMS, 8, length), f32),
            pltpu.VMEM((slabs, SUMS, 128), f32),
            pltpu.VMEM((depth, 2, width, length), f32),
            pltpu.VMEM((nodes, depth, 2, block, length), f32),
            pltpu.VMEM((nodes, 8, 128), f32),
            dma((3,)),
            dma((2,)),
            dma((2,)),
            dma((2,)),
            dma((2,)),
            dma((2,)),
            dma((2,)),
            dma((slabs,)),
            dma((slabs,)),
            dma((nodes,)),
            dma((nodes,)),
            dma((nodes, depth)),
            dma((nodes, depth)),
        ],
        compiler_params=pltpu.CompilerParams(
            collective_id=0, has_side_effects=True, vmem_limit_bytes=40 * 1024 * 1024
        ),
    )(
        warm_start,
        probes,
        potential,
        shift_points,
        quad_weights,
        jnp.asarray(ring_matrix(width, 0.0)),
        jnp.asarray(ring_matrix(length, -90.0)),
    )


def solution(mesh):
    return jax.shard_map(
        functools.partial(per_device, mesh.shape["node"], mesh.shape["grid"]),
        mesh=mesh,
        in_specs=(
            P(None, "grid", None, None),
            P("grid", None, None),
            P("node", None, None, "grid", None, None),
            P("node", None),
            P("node", None),
        ),
        out_specs=(P(None, None, None, "grid", "node", None), P()),
        check_vma=False,
    )
```

time: 310 us -> 91.2 us (0.29)
  blocking collectives: 84.1 us -> 0 us
  Pallas kernels: 0 us -> 81.8 us
  other arithmetic: 60.8 us -> 0 us
  between operations: 46.6 us -> 0.65 us
  local copies, waits for them, and re-layouts: 53.7 us -> 8.44 us
  matrix products: 29.6 us -> 0 us
  waiting for transfers between devices: 27.3 us -> 0 us
  starting transfers between devices: 5.97 us -> 0 us
    psum x4 -> x0, blocking collectives: 84.1 us -> none  [the longest x1 38.1 us: per_device(): trace_estimate = lax.psum(local_trace, ('node', 'grid'))]
    pallas_call x0 -> x1, Pallas kernels: none -> 81.8 us  [per_device(): pl.pallas_call(functools.partial(kernel, nodes, slabs), out_shape=(jax.Sh...]
    slice x31 -> x0, local copies, waits for them, and re-layouts: 44 us -> none  [the longest x6 14.3 us: hamiltonian_apply(): jnp.roll(middle, -2, 5)]
    dot_general x1 -> x0, matrix products: 29.6 us -> none  [per_device(): jnp.einsum('pzxy,spczxy->sc', probes, solution, precision=highest) / PROBES]
    add x5 -> x0, other arithmetic: 28.3 us -> none  [the longest x3 27.3 us: hamiltonian_apply(): near_weight * near_sum + far_weight * far_sum + self_weight * middle]
    ppermute x6 -> x0, waiting for transfers between devices: 27.3 us -> none  [the longest x3 21.4 us: with_halo(): lax.ppermute(head, axis, [((i + 1) % count, i) for i in range(count)])]
    another operation x10 -> x0, other arithmetic: 18.2 us -> none  [the longest x4 7 us: bilinear(): return jnp.stack([real_sum, imag_sum], axis=-1)]
    reduce_sum x5 -> x0, other arithmetic: 7.53 us -> none  [the longest x4 7.45 us: bilinear(): jnp.sum(first_vec[:, :, 0] * second_vec[:, :, 0] - first_vec[:, :, 1] * s...]
  transfers between devices with their start and end apart: 7 -> 0, of which waited for: 6 -> 0; matrix products, arithmetic and copies ran while one was open for 16% -> 0% of each run, Pallas kernels for 0% -> 0%
where the time goes in v1:
time: 91.2 us; the launch traced here: 90.9 us
  Pallas kernels  81.8 us (90%)
  local copies, waits for them, and re-layouts  8.44 us (9%)
    pallas_call x1, Pallas kernels, per_device(): pl.pallas_call(functools.partial(kernel, nodes, slabs), out_shape=(jax.Sh...  81.8 us
    unnamed x16, local copies, waits for them, and re-layouts  8.44 us

profile of v1, /device:TPU:0, one launch (start us, length us, event | category | flops | bytes accessed | tf_op | source)
XLA Modules:
  0.0 90.9 jit_solution(15740477636651636045)
XLA Ops:
  0.6 0.0 copy-start
  0.6 1.3 %copy-done = bf16[1,1,2,6,192,256]{5,4,3,2,1,0:T(8,128)(2,1)S(1)} copy-done((bf16[1,1,2,6,192,256]{5,4,3,2,1,0:T(8,128)(2,1)S(1)}, bf16[1,1,2,6,192,256]{5,4,3,2,1,0:T(8,128)(2,1)}, u32[]{:S(2)}) %copy-start) | copy-done | bytes 1179672
  1.9 0.0 copy-start.1
  1.9 1.3 %copy-done.1 = f32[1,6,192,256]{3,2,1,0:T(8,128)S(1)} copy-done((f32[1,6,192,256]{3,2,1,0:T(8,128)S(1)}, f32[1,6,192,256]{3,2,1,0:T(8,128)}, u32[]{:S(2)}) %copy-start.1) | copy-done | bytes 1179672
  3.2 0.0 copy-start.2
  3.2 1.3 %copy-done.2 = f32[6,192,256]{2,1,0:T(8,128)S(1)} copy-done((f32[6,192,256]{2,1,0:T(8,128)S(1)}, f32[6,192,256]{2,1,0:T(8,128)}, u32[]{:S(2)}) %copy-start.2) | copy-done | bytes 1179672
  4.4 0.0 copy-start.3
  4.4 0.9 copy-done.3
  5.3 0.0 copy-start.4
  5.4 0.9 copy-done.4
  6.2 0.0 copy-start.5
  6.2 0.7 copy-done.5
  6.9 0.0 copy-start.6
  6.9 0.7 copy-done.6
  7.6 81.8 %shard_map.86 = (f32[2,1,2,6,48,256]{5,4,3,2,1,0:T(8,128)S(1)}, f32[2]{0:T(128)S(1)}) custom-call(bf16[1,1,2,6,192,256]{5,4,3,2,1,0:T(8,128)(2,1)S(1)} %copy-done, f32[1,6,192,256]{3,2,1,0:T(8,128)S(1)} %copy-done.1, f32[6,192,256]{2,1,0:T(8,128)S(1)} %copy-done.2, f32[1,2]{1,0:T(1,128)S(1)} %copy-done.5, f32[1,2]{1,0:T(1,128)S(1)} %copy-done.6, ...), custom_call_target="tpu_custom_call" | custom-call | tf_op jit(solution)/shard_map/pallas_call | solution.py:411
  89.4 1.0 %copy.11 = f32[2,1,2,6,48,256]{5,4,3,2,1,0:T(8,128)} copy(f32[2,1,2,6,48,256]{5,4,3,2,1,0:T(8,128)S(1)} %get-tuple-element.4) | data formatting | bytes 2359296
  90.4 0.5 copy.12
Async XLA Ops:
  0.6 1.3 %copy-start = (bf16[1,1,2,6,192,256]{5,4,3,2,1,0:T(8,128)(2,1)S(1)}, bf16[1,1,2,6,192,256]{5,4,3,2,1,0:T(8,128)(2,1)}, u32[]{:S(2)}) copy-start(bf16[1,1,2,6,192,256]{5,4,3,2,1,0:T(8,128)(2,1)} %warm.1) | copy-start | bytes 3538948
  1.9 1.3 %copy-start.1 = (f32[1,6,192,256]{3,2,1,0:T(8,128)S(1)}, f32[1,6,192,256]{3,2,1,0:T(8,128)}, u32[]{:S(2)}) copy-start(f32[1,6,192,256]{3,2,1,0:T(8,128)} %probes.1) | copy-start | bytes 3538948
  3.2 1.3 %copy-start.2 = (f32[6,192,256]{2,1,0:T(8,128)S(1)}, f32[6,192,256]{2,1,0:T(8,128)}, u32[]{:S(2)}) copy-start(f32[6,192,256]{2,1,0:T(8,128)} %potential.1) | copy-start | bytes 3538948
  4.4 0.9 copy-start.3
  5.3 0.9 copy-start.4
  6.2 0.7 copy-start.5
  6.9 0.7 copy-start.6

commit v2 on v1

--- a/solution.py
+++ b/solution.py
@@ -44,10 +44,10 @@
     warm,
     probes,
     potential,
-    shift_ref,
-    weight_ref,
-    along_x,
-    along_y,
+    shift_hbm,
+    weight_hbm,
+    along_x_hbm,
+    along_y_hbm,
     moments,
     trace,
     xbuf,
@@ -55,13 +55,22 @@
     vbuf,
     rbuf,
     qbuf,
-    qlow,
     plane,
     acc,
     sums,
-    final,
-    arrived,
+    far_out,
+    far_in,
+    edge_out,
+    edge_in,
+    xwide,
+    peer_x,
+    peer_r,
+    peer_q,
     notes,
+    shift_ref,
+    weight_ref,
+    along_x,
+    along_y,
     local_sem,
     x_send,
     x_recv,
@@ -73,8 +82,10 @@
     s_recv,
     n_send,
     n_recv,
-    f_send,
-    f_recv,
+    g_send,
+    g_recv,
+    e_send,
+    e_recv,
 ):
     node, slab = lax.axis_index("node"), lax.axis_index("grid")
     depth, width, length = bbuf.shape
@@ -87,6 +98,10 @@
         pltpu.make_async_copy(warm.at[0, 0], xbuf.at[:, 2 : depth + 2], local_sem.at[0]),
         pltpu.make_async_copy(probes.at[0], bbuf, local_sem.at[1]),
         pltpu.make_async_copy(potential, vbuf, local_sem.at[2]),
+        pltpu.make_async_copy(shift_hbm, shift_ref, local_sem.at[3]),
+        pltpu.make_async_copy(weight_hbm, weight_ref, local_sem.at[4]),
+        pltpu.make_async_copy(along_x_hbm, along_x, local_sem.at[5]),
+        pltpu.make_async_copy(along_y_hbm, along_y, local_sem.at[6]),
     ]
     for load in loads:
         load.start()
@@ -119,11 +134,38 @@
     )
     x_up = send(warm.at[0, 0, :, depth - 2 : depth], xbuf.at[:, 0:2], x_send.at[1], x_recv.at[1], above)
 
+    groups = ((2, depth - 2), (0, 2), (depth - 2, depth))
+    early = {}
+
+    def share_rows(kind, source, target, offset, group):
+        first, last = groups[group]
+        slot = 3 * kind + group
+        step = 16 if block % 16 == 0 else 8
+        copies = []
+        for k in range(1, nodes):
+            peer = lax.rem(node + k, nodes)
+            rows = pl.ds(pl.multiple_of(peer * block, step), block)
+            copies.append(
+                send(
+                    source.at[:, first + offset : last + offset, rows, :],
+                    target.at[k, :, first:last],
+                    e_send.at[k, slot],
+                    e_recv.at[k, slot],
+                    (peer, slab),
+                )
+            )
+        early[kind, group] = copies
+
+    narrow = block % 16 == 0
+    if narrow:
+        for group in range(3):
+            share_rows(0, warm.at[0, 0], peer_x, 0, group)
+
     acc[...] = jnp.zeros_like(acc)
     qbuf[:, depth : depth + 2, half:, :] = jnp.zeros((2, 2, width - half, length), jnp.float32)
-    shift = shift_ref[0, 0], shift_ref[0, 1]
     for load in loads:
         load.wait()
+    shift = shift_ref[0, 0], shift_ref[0, 1]
 
     def dot(a, b):
         return jnp.dot(a, b, preferred_element_type=jnp.float32)
@@ -174,6 +216,9 @@
             source = bbuf[p, rows, :]
             image = apply(field, stencil, vbuf[p, rows, :])
             r = source - image[0], -image[1]
+            if not narrow:
+                for part in range(2):
+                    xwide[part, p, rows, :] = field[part]
             rbuf[0, p + 2, rows, :] = r[0]
             rbuf[1, p + 2, rows, :] = r[1]
             return (
@@ -229,35 +274,57 @@
         in_chunks(12, (terms, 2))
         return carry
 
+    def narrowed(source, target):
+        target[...] = source[...].astype(jnp.bfloat16)
+
+    def widened(source, target):
+        target[...] = source[...].astype(jnp.float32)
+
+    def shared(group):
+        if not narrow:
+            share_rows(0, xwide, peer_x, 0, group)
+        share_rows(1, rbuf, peer_r, 2, group)
+
     with jax.named_scope("residual"):
         lax.fori_loop(2, depth - 2, residual_plane, 0)
+        shared(0)
         x_up.wait_recv()
         x_down.wait_recv()
         lax.fori_loop(0, 2, residual_plane, 0)
-        r_down = send(
-            rbuf.at[:, 2:4], rbuf.at[:, depth + 2 : depth + 4], r_send.at[0], r_recv.at[0], below
+        near_down = send(
+            rbuf.at[:, 2], rbuf.at[:, depth + 2], r_send.at[0], r_recv.at[0], below
         )
+        narrowed(rbuf.at[:, 3], far_out.at[0])
+        far_down = send(far_out.at[0], far_in.at[0], g_send.at[0], g_recv.at[0], below)
         lax.fori_loop(depth - 2, depth, residual_plane, 0)
-        r_up = send(rbuf.at[:, depth : depth + 2], rbuf.at[:, 0:2], r_send.at[1], r_recv.at[1], above)
+        near_up = send(rbuf.at[:, depth + 1], rbuf.at[:, 1], r_send.at[1], r_recv.at[1], above)
+        narrowed(rbuf.at[:, depth], far_out.at[1])
+        far_up = send(far_out.at[1], far_in.at[1], g_send.at[1], g_recv.at[1], above)
+        shared(1)
+        shared(2)
 
     with jax.named_scope("image"):
         lax.fori_loop(2, depth - 2, image_plane, 0)
-        r_up.wait_recv()
+        share_rows(2, qbuf, peer_q, 0, 0)
+        near_up.wait_recv()
+        far_up.wait_recv()
+        widened(far_in.at[1], rbuf.at[:, 0])
         lax.fori_loop(0, 2, image_plane, 0)
-        q_down = send(
-            qbuf.at[:, 0:2, 0:half],
-            qbuf.at[:, depth : depth + 2, 0:half],
-            q_send.at[0],
-            q_recv.at[0],
-            below,
-        )
-        r_down.wait_recv()
+        narrowed(qbuf.at[:, 0:2, 0:half], edge_out.at[0])
+        q_down = send(edge_out.at[0], edge_in.at[0], q_send.at[0], q_recv.at[0], below)
+        near_down.wait_recv()
+        far_down.wait_recv()
+        widened(far_in.at[0], rbuf.at[:, depth + 3])
         lax.fori_loop(depth - 2, depth, image_plane, 0)
-        q_up = send(qbuf.at[:, depth - 2 : depth, half:width], qlow, q_send.at[1], q_recv.at[1], above)
+        narrowed(qbuf.at[:, depth - 2 : depth, half:width], edge_out.at[1])
+        q_up = send(edge_out.at[1], edge_in.at[1], q_send.at[1], q_recv.at[1], above)
+        share_rows(2, qbuf, peer_q, 0, 1)
+        share_rows(2, qbuf, peer_q, 0, 2)
 
     with jax.named_scope("energy"):
         lax.fori_loop(0, depth - 2, energy_plane, 0)
         q_down.wait_recv()
+        widened(edge_in.at[0], qbuf.at[:, depth : depth + 2, 0:half])
         lax.fori_loop(depth - 2, depth, energy_plane, 0)
         q_up.wait_recv()
 
@@ -265,8 +332,8 @@
             start = i * CHUNK
             mine = pl.ds(pl.multiple_of(half + start, CHUNK), CHUNK)
             theirs = pl.ds(pl.multiple_of(start, CHUNK), CHUNK)
-            near = [qlow[part, 1, theirs, :] for part in range(2)]
-            far = [qlow[part, 0, theirs, :] for part in range(2)]
+            near = [edge_in[1, part, 1, theirs, :].astype(jnp.float32) for part in range(2)]
+            far = [edge_in[1, part, 0, theirs, :].astype(jnp.float32) for part in range(2)]
             zeroth = [qbuf[part, 0, mine, :] for part in range(2)]
             first = [qbuf[part, 1, mine, :] for part in range(2)]
             one = cmul(zeroth, [32.0 * near[part] - 2.0 * far[part] for part in range(2)])
@@ -325,9 +392,9 @@
         weight = weight_ref[0, 0], weight_ref[0, 1]
         share = cmul(weight, inner)
         following = cmul(weight, ((shift[0] - 4.0) * 0.2, shift[1] * 0.2))
-        row = lax.broadcasted_iota(jnp.int32, (8, 128), 0)
-        note = jnp.zeros((8, 128), jnp.float32)
-        entries = (*weight, *following, share[0][:, 0:128], share[1][:, 0:128])
+        row = lax.broadcasted_iota(jnp.int32, (16, 128), 0)
+        note = jnp.zeros((16, 128), jnp.float32)
+        entries = (*weight, *following, *(v[:, 0:128] for v in (*share, *coef_r, *coef_q)))
         for i, entry in enumerate(entries):
             note = jnp.where(row == i, entry, note)
         notes[0] = note
@@ -336,75 +403,77 @@
             for k in range(1, nodes)
         ]
 
-    with jax.named_scope("solution_planes"):
-
-        def final_plane(p, carry):
-            def step(i, inner_carry):
-                rows = pl.ds(pl.multiple_of(i * CHUNK, CHUNK), CHUNK)
-                r = rbuf[0, p + 2, rows, :], rbuf[1, p + 2, rows, :]
-                q = qbuf[0, p, rows, :], qbuf[1, p, rows, :]
-                along_r, along_q = cmul(coef_r, r), cmul(coef_q, q)
-                for part in range(2):
-                    start = xbuf[part, p + 2, rows, :].astype(jnp.float32)
-                    final[p, part, rows, :] = start + along_r[part] + along_q[part]
-                return inner_carry
-
-            lax.fori_loop(0, width // CHUNK, step, 0)
-            return carry
-
-        final_copies = []
-        for p in range(depth):
-            final_plane(p, 0)
-            for k in range(1, nodes):
-                peer = lax.rem(node + k, nodes)
-                rows = pl.ds(pl.multiple_of(peer * block, 8), block)
-                final_copies.append(
-                    send(
-                        final.at[p, :, rows, :],
-                        arrived.at[k, p],
-                        f_send.at[k, p],
-                        f_recv.at[k, p],
-                        (peer, slab),
-                    )
-                )
-
     with jax.named_scope("moments"):
         for copy in note_copies:
             copy.wait_recv()
-        whole_trace = jnp.zeros((8, 128), jnp.float32)
+        whole_trace = jnp.zeros((16, 128), jnp.float32)
         for owner in range(nodes):
             whole_trace = whole_trace + notes[lax.rem(node - owner + nodes, nodes)]
-        lane = lax.broadcasted_iota(jnp.int32, (8, 128), 1)
+        lane = lax.broadcasted_iota(jnp.int32, (16, 128), 1)
         for part in range(2):
             trace[part] = jnp.sum(jnp.where((row == 4 + part) & (lane == 0), whole_trace, 0.0))
-        weights = []
+        factors = []
         for k in range(nodes):
-            wide = jnp.broadcast_to(jnp.sum(jnp.where(lane == 0, notes[k], 0.0), axis=1, keepdims=True), (8, length))
-            weights.append([(wide[i : i + 1], wide[i + 1 : i + 2]) for i in (0, 2)])
-        own = pl.ds(pl.multiple_of(node * block, 8), block)
-        for p in range(depth):
-            for copy in final_copies[p * (nodes - 1) : (p + 1) * (nodes - 1)]:
-                copy.wait_recv()
-            fields = [(final[p, 0, own, :], final[p, 1, own, :])]
-            for k in range(1, nodes):
-                fields.append((arrived[k, p, 0], arrived[k, p, 1]))
-            for degree in range(2):
-                terms = [cmul(weights[k][degree], fields[k]) for k in range(nodes)]
-                for part in range(2):
-                    value = terms[0][part]
-                    for term in terms[1:]:
-                        value = value + term[part]
-                    moments[degree, 0, part, p] = value
-
-    for copy in [x_down, x_up, r_down, r_up, q_down, q_up, *scalar_copies, *note_copies, *final_copies]:
+            first_lane = jnp.where(lane == 0, notes[k], 0.0)
+            wide = jnp.broadcast_to(jnp.sum(first_lane, axis=1, keepdims=True), (16, length))
+            factors.append([(wide[i : i + 1], wide[i + 1 : i + 2]) for i in (0, 2, 6, 8)])
+        piece = 16 if narrow else 8
+
+        def moment_plane(p, carry):
+            def step(i, inner_carry):
+                there = pl.ds(pl.multiple_of(i * piece, piece), piece)
+                here = pl.ds(pl.multiple_of(node * block + i * piece, piece), piece)
+                values = [None] * 4
+                for k in range(nodes):
+                    if k:
+                        x, r, q = (
+                            [ref[k, part, p, there, :] for part in range(2)]
+                            for ref in (peer_x, peer_r, peer_q)
+                        )
+                    else:
+                        if narrow:
+                            x = [xbuf[part, p + 2, here, :] for part in range(2)]
+                        else:
+                            x = [xwide[part, p, here, :] for part in range(2)]
+                        r = [rbuf[part, p + 2, here, :] for part in range(2)]
+                        q = [qbuf[part, p, here, :] for part in range(2)]
+                    along_r, along_q = cmul(factors[k][2], r), cmul(factors[k][3], q)
+                    field = [
+                        x[part].astype(jnp.float32) + along_r[part] + along_q[part]
+                        for part in range(2)
+                    ]
+                    for degree in range(2):
+                        term = cmul(factors[k][degree], field)
+                        for part in range(2):
+                            at = 2 * degree + part
+                            values[at] = term[part] if k == 0 else values[at] + term[part]
+                for degree in range(2):
+                    for part in range(2):
+                        moments[degree, 0, part, p, there, :] = values[2 * degree + part]
+                return inner_carry
+
+            lax.fori_loop(0, block // piece, step, 0)
+            return carry
+
+        for group, (first, last) in enumerate(groups):
+            for kind in range(3):
+                for copy in early[kind, group]:
+                    copy.wait_recv()
+            lax.fori_loop(first, last, moment_plane, 0)
+
+    early_copies = [copy for copies in early.values() for copy in copies]
+    for copy in [x_down, x_up, near_down, near_up, far_down, far_up, q_down, q_up]:
+        copy.wait_send()
+    for copy in [*scalar_copies, *note_copies, *early_copies]:
         copy.wait_send()
 
 
 def per_device(nodes, slabs, probes, potential, warm_start, shift_points, quad_weights):
     depth, width, length = potential.shape
     block = width // nodes
+    narrow = block % 16 == 0
     f32, bf16 = jnp.float32, jnp.bfloat16
-    anywhere = pl.BlockSpec(memory_space=pl.ANY)
+    anywhere = pl.BlockSpec(memory_space=pltpu.HBM)
     scalars = pl.BlockSpec(memory_space=pltpu.SMEM)
     vector = pl.BlockSpec(memory_space=pltpu.VMEM)
     dma = pltpu.SemaphoreType.DMA
@@ -414,7 +483,7 @@
             jax.ShapeDtypeStruct((2, 1, 2, depth, block, length), f32),
             jax.ShapeDtypeStruct((2,), f32),
         ),
-        in_specs=[anywhere, anywhere, anywhere, scalars, scalars, vector, vector],
+        in_specs=[anywhere] * 7,
         out_specs=(vector, scalars),
         scratch_shapes=[
             pltpu.VMEM((2, depth + 4, width, length), bf16),
@@ -422,14 +491,23 @@
             pltpu.VMEM((depth, width, length), f32),
             pltpu.VMEM((2, depth + 4, width, length), f32),
             pltpu.VMEM((2, depth + 2, width, length), f32),
-            pltpu.VMEM((2, 2, width - width // 2, length), f32),
             pltpu.VMEM((2, width, length), f32),
             pltpu.VMEM((SUMS, 8, length), f32),
             pltpu.VMEM((slabs, SUMS, 128), f32),
-            pltpu.VMEM((depth, 2, width, length), f32),
-            pltpu.VMEM((nodes, depth, 2, block, length), f32),
-            pltpu.VMEM((nodes, 8, 128), f32),
-            dma((3,)),
+            pltpu.VMEM((2, 2, width, length), bf16),
+            pltpu.VMEM((2, 2, width, length), bf16),
+            pltpu.VMEM((2, 2, 2, width // 2, length), bf16),
+            pltpu.VMEM((2, 2, 2, width // 2, length), bf16),
+            pltpu.VMEM((8, 128) if narrow else (2, depth, width, length), f32),
+            pltpu.VMEM((nodes, 2, depth, block, length), bf16 if narrow else f32),
+            pltpu.VMEM((nodes, 2, depth, block, length), f32),
+            pltpu.VMEM((nodes, 2, depth, block, length), f32),
+            pltpu.VMEM((nodes, 16, 128), f32),
+            pltpu.SMEM((1, 2), f32),
+            pltpu.SMEM((1, 2), f32),
+            pltpu.VMEM((width, width), bf16),
+            pltpu.VMEM((length, length), bf16),
+            dma((7,)),
             dma((2,)),
             dma((2,)),
             dma((2,)),
@@ -440,8 +518,10 @@
             dma((slabs,)),
             dma((nodes,)),
             dma((nodes,)),
-            dma((nodes, depth)),
-            dma((nodes, depth)),
+            dma((2,)),
+            dma((2,)),
+            dma((nodes, 9)),
+            dma((nodes, 9)),
         ],
         compiler_params=pltpu.CompilerParams(
             collective_id=0, has_side_effects=True, vmem_limit_bytes=40 * 1024 * 1024

time: 91.2 us -> 86.1 us (0.944)
  Pallas kernels: 81.8 us -> 76.7 us
    pallas_call x1, Pallas kernels: 81.8 us -> 76.7 us  [per_device(): pl.pallas_call(functools.partial(kernel, nodes, slabs), out_shape=(jax.Sh...]
where the time goes in v2:
time: 86.1 us; the launch traced here: 85.8 us
  Pallas kernels  76.7 us (89%)
  local copies, waits for them, and re-layouts  8.44 us (10%)
    pallas_call x1, Pallas kernels, per_device(): pl.pallas_call(functools.partial(kernel, nodes, slabs), out_shape=(jax.Sh...  76.7 us
    unnamed x16, local copies, waits for them, and re-layouts  8.44 us

profile of v2, /device:TPU:0, one launch (start us, length us, event | category | flops | bytes accessed | tf_op | source)
XLA Modules:
  0.0 85.8 jit_solution(1747573603727827399)
XLA Ops:
  0.6 0.0 copy-start
  0.6 1.3 %copy-done = bf16[1,1,2,6,192,256]{5,4,3,2,1,0:T(8,128)(2,1)S(1)} copy-done((bf16[1,1,2,6,192,256]{5,4,3,2,1,0:T(8,128)(2,1)S(1)}, bf16[1,1,2,6,192,256]{5,4,3,2,1,0:T(8,128)(2,1)}, u32[]{:S(2)}) %copy-start) | copy-done | bytes 1179672
  1.9 0.0 copy-start.1
  1.9 1.3 %copy-done.1 = f32[1,6,192,256]{3,2,1,0:T(8,128)S(1)} copy-done((f32[1,6,192,256]{3,2,1,0:T(8,128)S(1)}, f32[1,6,192,256]{3,2,1,0:T(8,128)}, u32[]{:S(2)}) %copy-start.1) | copy-done | bytes 1179672
  3.2 0.0 copy-start.2
  3.2 1.3 %copy-done.2 = f32[6,192,256]{2,1,0:T(8,128)S(1)} copy-done((f32[6,192,256]{2,1,0:T(8,128)S(1)}, f32[6,192,256]{2,1,0:T(8,128)}, u32[]{:S(2)}) %copy-start.2) | copy-done | bytes 1179672
  4.4 0.0 copy-start.3
  4.4 0.9 %copy-done.3 = bf16[256,256]{1,0:T(8,128)(2,1)S(1)} copy-done((bf16[256,256]{1,0:T(8,128)(2,1)S(1)}, bf16[256,256]{1,0:T(8,128)(2,1)}, u32[]{:S(2)}) %copy-start.3) | copy-done | bytes 131096
  5.3 0.0 copy-start.4
  5.4 0.9 %copy-done.4 = bf16[192,192]{1,0:T(8,128)(2,1)S(1)} copy-done((bf16[192,192]{1,0:T(8,128)(2,1)S(1)}, bf16[192,192]{1,0:T(8,128)(2,1)}, u32[]{:S(2)}) %copy-start.4) | copy-done | bytes 73752
  6.2 0.0 copy-start.5
  6.2 0.7 copy-done.5
  6.9 0.0 copy-start.6
  6.9 0.7 copy-done.6
  7.6 76.7 %shard_map.86 = (f32[2,1,2,6,48,256]{5,4,3,2,1,0:T(8,128)S(1)}, f32[2]{0:T(128)S(1)}) custom-call(bf16[1,1,2,6,192,256]{5,4,3,2,1,0:T(8,128)(2,1)S(1)} %copy-done, f32[1,6,192,256]{3,2,1,0:T(8,128)S(1)} %copy-done.1, f32[6,192,256]{2,1,0:T(8,128)S(1)} %copy-done.2, f32[1,2]{1,0:T(1,128)S(1)} %copy-done.5, f32[1,2]{1,0:T(1,128)S(1)} %copy-done.6, ...), custom_call_target="tpu_custom_call" | custom-call | tf_op jit(solution)/shard_map/pallas_call | solution.py:480
  84.3 1.0 %copy.11 = f32[2,1,2,6,48,256]{5,4,3,2,1,0:T(8,128)} copy(f32[2,1,2,6,48,256]{5,4,3,2,1,0:T(8,128)S(1)} %get-tuple-element.4) | data formatting | bytes 2359296
  85.3 0.5 copy.12
Async XLA Ops:
  0.6 1.3 %copy-start = (bf16[1,1,2,6,192,256]{5,4,3,2,1,0:T(8,128)(2,1)S(1)}, bf16[1,1,2,6,192,256]{5,4,3,2,1,0:T(8,128)(2,1)}, u32[]{:S(2)}) copy-start(bf16[1,1,2,6,192,256]{5,4,3,2,1,0:T(8,128)(2,1)} %warm.1) | copy-start | bytes 3538948
  1.9 1.3 %copy-start.1 = (f32[1,6,192,256]{3,2,1,0:T(8,128)S(1)}, f32[1,6,192,256]{3,2,1,0:T(8,128)}, u32[]{:S(2)}) copy-start(f32[1,6,192,256]{3,2,1,0:T(8,128)} %probes.1) | copy-start | bytes 3538948
  3.2 1.3 %copy-start.2 = (f32[6,192,256]{2,1,0:T(8,128)S(1)}, f32[6,192,256]{2,1,0:T(8,128)}, u32[]{:S(2)}) copy-start(f32[6,192,256]{2,1,0:T(8,128)} %potential.1) | copy-start | bytes 3538948
  4.4 0.9 %copy-start.3 = (bf16[256,256]{1,0:T(8,128)(2,1)S(1)}, bf16[256,256]{1,0:T(8,128)(2,1)}, u32[]{:S(2)}) copy-start(bf16[256,256]{1,0:T(8,128)(2,1)} %constant.5.clone.along_y_hbm) | copy-start | bytes 393220
  5.3 0.9 %copy-start.4 = (bf16[192,192]{1,0:T(8,128)(2,1)S(1)}, bf16[192,192]{1,0:T(8,128)(2,1)}, u32[]{:S(2)}) copy-start(bf16[192,192]{1,0:T(8,128)(2,1)} %constant.4.clone.along_x_hbm) | copy-start | bytes 221188
  6.2 0.7 copy-start.5
  6.9 0.7 copy-start.6

commit v3 on v2

--- a/solution.py
+++ b/solution.py
@@ -66,6 +66,8 @@
     peer_x,
     peer_r,
     peer_q,
+    late,
+    peer_late,
     notes,
     shift_ref,
     weight_ref,
@@ -139,7 +141,7 @@
 
     def share_rows(kind, source, target, offset, group):
         first, last = groups[group]
-        slot = 3 * kind + group
+        slot = 2 * kind + group
         step = 16 if block % 16 == 0 else 8
         copies = []
         for k in range(1, nodes):
@@ -158,7 +160,7 @@
 
     narrow = block % 16 == 0
     if narrow:
-        for group in range(3):
+        for group in range(2):
             share_rows(0, warm.at[0, 0], peer_x, 0, group)
 
     acc[...] = jnp.zeros_like(acc)
@@ -301,7 +303,6 @@
         narrowed(rbuf.at[:, depth], far_out.at[1])
         far_up = send(far_out.at[1], far_in.at[1], g_send.at[1], g_recv.at[1], above)
         shared(1)
-        shared(2)
 
     with jax.named_scope("image"):
         lax.fori_loop(2, depth - 2, image_plane, 0)
@@ -319,7 +320,6 @@
         narrowed(qbuf.at[:, depth - 2 : depth, half:width], edge_out.at[1])
         q_up = send(edge_out.at[1], edge_in.at[1], q_send.at[1], q_recv.at[1], above)
         share_rows(2, qbuf, peer_q, 0, 1)
-        share_rows(2, qbuf, peer_q, 0, 2)
 
     with jax.named_scope("energy"):
         lax.fori_loop(0, depth - 2, energy_plane, 0)
@@ -404,6 +404,36 @@
         ]
 
     with jax.named_scope("moments"):
+        late_first = depth - 2
+        late_copies = []
+
+        def late_plane(p):
+            def step(i, carry):
+                rows = pl.ds(pl.multiple_of(i * CHUNK, CHUNK), CHUNK)
+                r = rbuf[0, p + 2, rows, :], rbuf[1, p + 2, rows, :]
+                q = qbuf[0, p, rows, :], qbuf[1, p, rows, :]
+                along_r, along_q = cmul(coef_r, r), cmul(coef_q, q)
+                for part in range(2):
+                    start = xbuf[part, p + 2, rows, :].astype(jnp.float32)
+                    late[p - late_first, part, rows, :] = start + along_r[part] + along_q[part]
+                return carry
+
+            lax.fori_loop(0, width // CHUNK, step, 0)
+
+        for p in range(late_first, depth):
+            late_plane(p)
+            for k in range(1, nodes):
+                peer = lax.rem(node + k, nodes)
+                late_copies.append(
+                    send(
+                        late.at[p - late_first, :, pl.ds(pl.multiple_of(peer * block, 8), block), :],
+                        peer_late.at[k, p - late_first],
+                        e_send.at[k, 6 + p - late_first],
+                        e_recv.at[k, 6 + p - late_first],
+                        (peer, slab),
+                    )
+                )
+
         for copy in note_copies:
             copy.wait_recv()
         whole_trace = jnp.zeros((16, 128), jnp.float32)
@@ -418,6 +448,29 @@
             wide = jnp.broadcast_to(jnp.sum(first_lane, axis=1, keepdims=True), (16, length))
             factors.append([(wide[i : i + 1], wide[i + 1 : i + 2]) for i in (0, 2, 6, 8)])
         piece = 16 if narrow else 8
+
+        def late_moment_plane(at, carry):
+            def step(i, inner_carry):
+                there = pl.ds(pl.multiple_of(i * piece, piece), piece)
+                here = pl.ds(pl.multiple_of(node * block + i * piece, piece), piece)
+                values = [None] * 4
+                for k in range(nodes):
+                    if k:
+                        field = [peer_late[k, at, part, there, :] for part in range(2)]
+                    else:
+                        field = [late[at, part, here, :] for part in range(2)]
+                    for degree in range(2):
+                        term = cmul(factors[k][degree], field)
+                        for part in range(2):
+                            n = 2 * degree + part
+                            values[n] = term[part] if k == 0 else values[n] + term[part]
+                for degree in range(2):
+                    for part in range(2):
+                        moments[degree, 0, part, late_first + at, there, :] = values[2 * degree + part]
+                return inner_carry
+
+            lax.fori_loop(0, block // piece, step, 0)
+            return carry
 
         def moment_plane(p, carry):
             def step(i, inner_carry):
@@ -455,13 +508,18 @@
             lax.fori_loop(0, block // piece, step, 0)
             return carry
 
-        for group, (first, last) in enumerate(groups):
+        for group, (first, last) in enumerate(groups[:2]):
             for kind in range(3):
                 for copy in early[kind, group]:
                     copy.wait_recv()
             lax.fori_loop(first, last, moment_plane, 0)
 
-    early_copies = [copy for copies in early.values() for copy in copies]
+        for at in range(2):
+            for copy in late_copies[at * (nodes - 1) : (at + 1) * (nodes - 1)]:
+                copy.wait_recv()
+            late_moment_plane(at, 0)
+
+    early_copies = late_copies + [copy for copies in early.values() for copy in copies]
     for copy in [x_down, x_up, near_down, near_up, far_down, far_up, q_down, q_up]:
         copy.wait_send()
     for copy in [*scalar_copies, *note_copies, *early_copies]:
@@ -502,6 +560,8 @@
             pltpu.VMEM((nodes, 2, depth, block, length), bf16 if narrow else f32),
             pltpu.VMEM((nodes, 2, depth, block, length), f32),
             pltpu.VMEM((nodes, 2, depth, block, length), f32),
+            pltpu.VMEM((2, 2, width, length), f32),
+            pltpu.VMEM((nodes, 2, 2, block, length), f32),
             pltpu.VMEM((nodes, 16, 128), f32),
             pltpu.SMEM((1, 2), f32),
             pltpu.SMEM((1, 2), f32),
@@ -520,11 +580,11 @@
             dma((nodes,)),
             dma((2,)),
             dma((2,)),
-            dma((nodes, 9)),
-            dma((nodes, 9)),
+            dma((nodes, 8)),
+            dma((nodes, 8)),
         ],
         compiler_params=pltpu.CompilerParams(
-            collective_id=0, has_side_effects=True, vmem_limit_bytes=40 * 1024 * 1024
+            collective_id=0, has_side_effects=True, vmem_limit_bytes=64 * 1024 * 1024
         ),
     )(
         warm_start,

time: 86.1 us -> 64.9 us (0.75)
  Pallas kernels: 76.7 us -> 61.2 us
  local copies, waits for them, and re-layouts: 8.44 us -> 2.9 us
    pallas_call x1, Pallas kernels: 76.7 us -> 61.2 us  [per_device(): pl.pallas_call(functools.partial(kernel, nodes, slabs), out_shape=(jax.Sh...]
    unnamed x16 -> x4, local copies, waits for them, and re-layouts: 8.44 us -> 2.9 us
where the time goes in v3:
time: 64.9 us; the launch traced here: 64.8 us
  Pallas kernels  61.2 us (94%)
  local copies, waits for them, and re-layouts  2.9 us (4%)
  between operations  0.65 us (1%)
    pallas_call x1, Pallas kernels, per_device(): pl.pallas_call(functools.partial(kernel, nodes, slabs), out_shape=(jax.Sh...  61.2 us
    unnamed x4, local copies, waits for them, and re-layouts  2.9 us

profile of v3, /device:TPU:0, one launch (start us, length us, event | category | flops | bytes accessed | tf_op | source)
XLA Modules:
  0.0 64.8 jit_solution(4097163864782787271)
XLA Ops:
  0.6 61.2 %shard_map.86 = (f32[2,1,2,6,48,256]{5,4,3,2,1,0:T(8,128)}, f32[2]{0:T(128)}) custom-call(bf16[1,1,2,6,192,256]{5,4,3,2,1,0:T(8,128)(2,1)} %warm.1, f32[1,6,192,256]{3,2,1,0:T(8,128)} %probes.1, f32[6,192,256]{2,1,0:T(8,128)} %potential.1, f32[1,2]{1,0:T(1,128)} %shift_hbm.1, f32[1,2]{1,0:T(1,128)} %weight_hbm.1, ...), custom_call_target="tpu_custom_call" | custom-call | tf_op jit(solution)/shard_map/pallas_call | solution.py:538
  61.8 0.0 copy-start
  61.9 2.4 %copy.11 = f32[2,1,2,6,48,256]{5,4,3,2,1,0:T(8,128)} copy(f32[2,1,2,6,48,256]{5,4,3,2,1,0:T(8,128)} %get-tuple-element.4) | data formatting | bytes 2359296
  64.2 0.0 copy-done
  64.2 0.5 copy.12
Async XLA Ops:
  61.8 2.4 %copy-start = (f32[2]{0:T(128)S(1)}, f32[2]{0:T(128)}, u32[]{:S(2)}) copy-start(f32[2]{0:T(128)} %get-tuple-element.5) | copy-start | bytes 28

commit v4 on v3

--- a/solution.py
+++ b/solution.py
@@ -291,15 +291,17 @@
         lax.fori_loop(2, depth - 2, residual_plane, 0)
         shared(0)
         x_up.wait_recv()
-        x_down.wait_recv()
-        lax.fori_loop(0, 2, residual_plane, 0)
+        lax.fori_loop(0, 1, residual_plane, 0)
         near_down = send(
             rbuf.at[:, 2], rbuf.at[:, depth + 2], r_send.at[0], r_recv.at[0], below
         )
+        lax.fori_loop(1, 2, residual_plane, 0)
         narrowed(rbuf.at[:, 3], far_out.at[0])
         far_down = send(far_out.at[0], far_in.at[0], g_send.at[0], g_recv.at[0], below)
-        lax.fori_loop(depth - 2, depth, residual_plane, 0)
+        x_down.wait_recv()
+        lax.fori_loop(depth - 1, depth, residual_plane, 0)
         near_up = send(rbuf.at[:, depth + 1], rbuf.at[:, 1], r_send.at[1], r_recv.at[1], above)
+        lax.fori_loop(depth - 2, depth - 1, residual_plane, 0)
         narrowed(rbuf.at[:, depth], far_out.at[1])
         far_up = send(far_out.at[1], far_in.at[1], g_send.at[1], g_recv.at[1], above)
         shared(1)

time: 64.9 us -> 64.9 us (level)
  no operation moved by 1% of the time
where the time goes in v4:
time: 64.9 us; the launch traced here: 64.8 us
  Pallas kernels  61.2 us (94%)
  local copies, waits for them, and re-layouts  2.9 us (4%)
  between operations  0.65 us (1%)
    pallas_call x1, Pallas kernels, per_device(): pl.pallas_call(functools.partial(kernel, nodes, slabs), out_shape=(jax.Sh...  61.2 us
    unnamed x4, local copies, waits for them, and re-layouts  2.9 us

profile of v4, /device:TPU:0, one launch (start us, length us, event | category | flops | bytes accessed | tf_op | source)
XLA Modules:
  0.0 64.8 jit_solution(10923985028895480696)
XLA Ops:
  0.6 61.2 %shard_map.86 = (f32[2,1,2,6,48,256]{5,4,3,2,1,0:T(8,128)}, f32[2]{0:T(128)}) custom-call(bf16[1,1,2,6,192,256]{5,4,3,2,1,0:T(8,128)(2,1)} %warm.1, f32[1,6,192,256]{3,2,1,0:T(8,128)} %probes.1, f32[6,192,256]{2,1,0:T(8,128)} %potential.1, f32[1,2]{1,0:T(1,128)} %shift_hbm.1, f32[1,2]{1,0:T(1,128)} %weight_hbm.1, ...), custom_call_target="tpu_custom_call" | custom-call | tf_op jit(solution)/shard_map/pallas_call | solution.py:540
  61.8 0.0 copy-start
  61.9 2.4 %copy.11 = f32[2,1,2,6,48,256]{5,4,3,2,1,0:T(8,128)} copy(f32[2,1,2,6,48,256]{5,4,3,2,1,0:T(8,128)} %get-tuple-element.4) | data formatting | bytes 2359296
  64.2 0.0 copy-done
  64.2 0.5 copy.12
Async XLA Ops:
  61.8 2.4 %copy-start = (f32[2]{0:T(128)S(1)}, f32[2]{0:T(128)}, u32[]{:S(2)}) copy-start(f32[2]{0:T(128)} %get-tuple-element.5) | copy-start | bytes 28

commit v5 on v3

--- a/solution.py
+++ b/solution.py
@@ -136,7 +136,7 @@
     )
     x_up = send(warm.at[0, 0, :, depth - 2 : depth], xbuf.at[:, 0:2], x_send.at[1], x_recv.at[1], above)
 
-    groups = ((2, depth - 2), (0, 2), (depth - 2, depth))
+    groups = ((2, depth - 3), (0, 2))
     early = {}
 
     def share_rows(kind, source, target, offset, group):
@@ -404,7 +404,7 @@
         ]
 
     with jax.named_scope("moments"):
-        late_first = depth - 2
+        late_first = depth - 3
         late_copies = []
 
         def late_plane(p):
@@ -508,13 +508,13 @@
             lax.fori_loop(0, block // piece, step, 0)
             return carry
 
-        for group, (first, last) in enumerate(groups[:2]):
+        for group, (first, last) in enumerate(groups):
             for kind in range(3):
                 for copy in early[kind, group]:
                     copy.wait_recv()
             lax.fori_loop(first, last, moment_plane, 0)
 
-        for at in range(2):
+        for at in range(3):
             for copy in late_copies[at * (nodes - 1) : (at + 1) * (nodes - 1)]:
                 copy.wait_recv()
             late_moment_plane(at, 0)
@@ -560,8 +560,8 @@
             pltpu.VMEM((nodes, 2, depth, block, length), bf16 if narrow else f32),
             pltpu.VMEM((nodes, 2, depth, block, length), f32),
             pltpu.VMEM((nodes, 2, depth, block, length), f32),
-            pltpu.VMEM((2, 2, width, length), f32),
-            pltpu.VMEM((nodes, 2, 2, block, length), f32),
+            pltpu.VMEM((3, 2, width, length), f32),
+            pltpu.VMEM((nodes, 3, 2, block, length), f32),
             pltpu.VMEM((nodes, 16, 128), f32),
             pltpu.SMEM((1, 2), f32),
             pltpu.SMEM((1, 2), f32),
@@ -580,8 +580,8 @@
             dma((nodes,)),
             dma((2,)),
             dma((2,)),
-            dma((nodes, 8)),
-            dma((nodes, 8)),
+            dma((nodes, 9)),
+            dma((nodes, 9)),
         ],
         compiler_params=pltpu.CompilerParams(
             collective_id=0, has_side_effects=True, vmem_limit_bytes=64 * 1024 * 1024

time: 64.9 us -> 64.1 us (0.988)
  Pallas kernels: 61.2 us -> 60.4 us
    pallas_call x1, Pallas kernels: 61.2 us -> 60.4 us  [per_device(): pl.pallas_call(functools.partial(kernel, nodes, slabs), out_shape=(jax.Sh...]
where the time goes in v5:
time: 64.1 us; the launch traced here: 64 us
  Pallas kernels  60.4 us (94%)
  local copies, waits for them, and re-layouts  2.9 us (5%)
  between operations  0.65 us (1%)
    pallas_call x1, Pallas kernels, per_device(): pl.pallas_call(functools.partial(kernel, nodes, slabs), out_shape=(jax.Sh...  60.4 us
    unnamed x4, local copies, waits for them, and re-layouts  2.9 us

profile of v5, /device:TPU:0, one launch (start us, length us, event | category | flops | bytes accessed | tf_op | source)
XLA Modules:
  0.0 64.0 jit_solution(9525886012665301437)
XLA Ops:
  0.6 60.4 %shard_map.86 = (f32[2,1,2,6,48,256]{5,4,3,2,1,0:T(8,128)}, f32[2]{0:T(128)}) custom-call(bf16[1,1,2,6,192,256]{5,4,3,2,1,0:T(8,128)(2,1)} %warm.1, f32[1,6,192,256]{3,2,1,0:T(8,128)} %probes.1, f32[6,192,256]{2,1,0:T(8,128)} %potential.1, f32[1,2]{1,0:T(1,128)} %shift_hbm.1, f32[1,2]{1,0:T(1,128)} %weight_hbm.1, ...), custom_call_target="tpu_custom_call" | custom-call | tf_op jit(solution)/shard_map/pallas_call | solution.py:538
  61.0 0.0 copy-start
  61.1 2.4 %copy.11 = f32[2,1,2,6,48,256]{5,4,3,2,1,0:T(8,128)} copy(f32[2,1,2,6,48,256]{5,4,3,2,1,0:T(8,128)} %get-tuple-element.4) | data formatting | bytes 2359296
  63.4 0.0 copy-done
  63.4 0.5 copy.12
Async XLA Ops:
  61.0 2.4 %copy-start = (f32[2]{0:T(128)S(1)}, f32[2]{0:T(128)}, u32[]{:S(2)}) copy-start(f32[2]{0:T(128)} %get-tuple-element.5) | copy-start | bytes 28
